TPU v7x, 256 devices: a whole 4x4x8 slice. The times are simulated.
256 devices in a mesh: dp: 32 (over z, y_hi, core), ctx: 8 (over x, y_lo).
Axes of the slice: x: 4, y: 4 (y_hi: 2, y_lo: 2; y = y_hi * 2 + y_lo), z: 8, core: 2. Of those that a mesh axis runs over, the one named last changes fastest.
Arguments:
- q_heads: bfloat16 [32, 1536, 2048], P('dp', 'ctx'), may hold values from -8 to 8
- keys: bfloat16 [32, 1536, 128], P('dp', 'ctx'), may hold values from -8 to 8
- values: bfloat16 [32, 1536, 128], P('dp', 'ctx'), may hold values from -6 to 6
- out_grad: bfloat16 [32, 1536, 2048], P('dp', 'ctx'), may hold values from -0.29882812 to 0.29882812
- hidden_in: bfloat16 [32, 1536, 16384], P('dp', 'ctx'), may hold values from -6 to 6
- doc_lengths: int32 [32, 8], P('dp'), may hold values from 1 to 576, 1536 in all within a row
- span_order: int32 [16], replicated, may hold values from 0 to 15, each once
- m_codes: int32 [16384, 256], P('dp'), may hold values from -127 to 127
- m_scales: float32 [2048], P('dp'), may hold values from 0.05 to 0.5
- v_codes: int32 [16384, 256], P('dp'), may hold values from 1 to 255
- v_scales: float32 [2048], P('dp'), may hold values from 0.05 to 1
Outputs:
- dq: bfloat16 [32, 1536, 2048], P('dp', 'ctx')
- update: float32 [16384, 256], P('dp')
- m_norm: float32 [16384, 256], P('dp')
- m_absmax: float32 [2048], P('dp')
- v_norm: float32 [16384, 256], P('dp')
- v_absmax: float32 [2048], P('dp')
Inputs may be any that keep to these rules, and one draw needn't show every extreme that they name: `doc_lengths`: each sequence's 8 lengths sum to 1536. `span_order`: each stored block names a different position block.
All inputs are finite; a program needn't handle non-finite values. Where the computation divides by a largest or mean magnitude, that divisor is 1e-20 or more.
Results may differ from a plain program's by a relative error of at most 0.0078.
Values may be sent and summed in bfloat16 or wider, within the bound.
A program may use at most 128 MiB of HBM per device.

v0:
```python
import math
import jax
import jax.numpy as jnp
from jax import lax
from jax.sharding import PartitionSpec as P

BLOCK = 2048
STEP = 10


def positions(order, span, total):
    rows = jnp.arange(total, dtype=jnp.int32)
    slot = rows // span
    match = slot[:, None] == jnp.arange(order.shape[0], dtype=jnp.int32)[None, :]
    first = jnp.sum(jnp.where(match, order[None, :], 0), axis=1)
    return first * span + rows % span


def documents(pos, lengths):
    ends = jnp.cumsum(lengths)
    return jnp.sum((pos[:, None] >= ends[None, :]).astype(jnp.int32), axis=1)


def adam_blocks(grad, m_codes, m_scales, v_codes, v_scales):
    shape = grad.shape
    g_blocks = grad.reshape(-1, BLOCK)
    m_old = m_codes.reshape(-1, BLOCK).astype(jnp.float32) / 127.0 * m_scales[:, None]
    v_old = v_codes.reshape(-1, BLOCK).astype(jnp.float32) / 255.0 * v_scales[:, None]
    moment = 0.9 * m_old + 0.1 * g_blocks
    second = 0.95 * v_old + 0.05 * g_blocks * g_blocks
    update = moment / (1.0 - 0.9**STEP) / (jnp.sqrt(second / (1.0 - 0.95**STEP)) + 1e-08)
    m_absmax = jnp.max(jnp.abs(moment), axis=1)
    v_absmax = jnp.max(second, axis=1)
    m_norm = moment / (m_absmax[:, None] + 1e-06)
    v_norm = second / (v_absmax[:, None] + 1e-06)
    return (update.reshape(shape), m_norm.reshape(shape), m_absmax, v_norm.reshape(shape), v_absmax)


def contract_rows(left, right):
    return lax.dot_general(
        left, right, (((0,), (0,)), ((), ())), preferred_element_type=jnp.float32
    )


def contract_cols(left, right):
    return lax.dot_general(
        left, right, (((1,), (1,)), ((), ())), preferred_element_type=jnp.float32
    )


def shards(
    q_heads,
    keys,
    values,
    out_grad,
    hidden_in,
    doc_lengths,
    span_order,
    m_codes,
    m_scales,
    v_codes,
    v_scales,
):
    rows = q_heads.shape[1]
    head_dim = keys.shape[2]
    heads_width = q_heads.shape[2]
    nheads = heads_width // head_dim
    scale = 1.0 / math.sqrt(head_dim)
    total = rows * lax.axis_size("ctx")
    key_all, value_all = (
        lax.all_gather(keys[0], "ctx", axis=0, tiled=True),
        lax.all_gather(values[0], "ctx", axis=0, tiled=True),
    )
    pos = positions(span_order, rows // 2, total)
    doc = documents(pos, doc_lengths[0])
    first_row = lax.axis_index("ctx") * rows
    query_pos = lax.dynamic_slice_in_dim(pos, first_row, rows)
    query_doc = lax.dynamic_slice_in_dim(doc, first_row, rows)
    queries = q_heads[0].reshape(rows * nheads, head_dim)
    grads_out = out_grad[0].reshape(rows * nheads, head_dim)
    width = min(512, total)
    nblocks = total // width
    blocks = (
        key_all.reshape(nblocks, width, head_dim),
        value_all.reshape(nblocks, width, head_dim),
        pos.reshape(nblocks, width),
        doc.reshape(nblocks, width),
    )

    def block_masks(key_pos, key_doc):
        small = (key_pos[None, :] <= query_pos[:, None]) & (key_doc[None, :] == query_doc[:, None])
        wide = jnp.broadcast_to(small[:, None, :], (rows, nheads, width)).reshape(
            rows * nheads, width
        )
        return (small, wide)

    def forward_terms(carry, block):
        key_block, value_block, key_pos, key_doc = block
        small, wide = block_masks(key_pos, key_doc)
        top, denom, weighted = carry
        scores = contract_cols(queries, key_block) * scale
        dprob = contract_cols(grads_out, value_block)
        new_top = jnp.maximum(top, jnp.max(jnp.where(wide, scores, -1e30), axis=1, keepdims=True))
        expo = jnp.where(wide, jnp.exp(scores - new_top), 0.0)
        factor = jnp.exp(top - new_top)
        result = (
            new_top,
            denom * factor + jnp.sum(expo, axis=1, keepdims=True),
            weighted * factor + jnp.sum(expo * dprob, axis=1, keepdims=True),
        )
        return (result, None)

    column = jnp.zeros((rows * nheads, 1), jnp.float32)
    start_state = (column - 1e30, column, column)
    (top, denom, weighted), unused = lax.scan(forward_terms, start_state, blocks)
    delta = weighted / denom

    def backward_terms(accum, block):
        key_block, value_block, key_pos, key_doc = block
        small, wide = block_masks(key_pos, key_doc)
        acc = accum
        scores = contract_cols(queries, key_block) * scale
        dprob = contract_cols(grads_out, value_block)
        prob = jnp.where(wide, jnp.exp(scores - top), 0.0) / denom
        prob_low = prob.astype(jnp.bfloat16)
        dscore = (prob * (dprob - delta)).astype(jnp.bfloat16)
        acc = acc + jnp.dot(dscore, key_block, preferred_element_type=jnp.float32)
        dkey = contract_rows(dscore, queries) * scale
        dvalue = contract_rows(prob_low, grads_out)
        return (acc, jnp.concatenate([dkey, dvalue], axis=1))

    dq_sum, pieces = lax.scan(
        backward_terms, jnp.zeros((rows * nheads, head_dim), jnp.float32), blocks
    )
    dq = (dq_sum * scale).reshape(1, rows, heads_width).astype(jnp.bfloat16)
    partial_grads = pieces.reshape(total, 2 * head_dim)
    own = lax.psum_scatter(partial_grads, "ctx", scatter_dimension=0, tiled=True)
    own_low = own.astype(jnp.bfloat16)
    layer_in = hidden_in[0]
    grad = lax.psum_scatter(contract_rows(layer_in, own_low), "dp", scatter_dimension=0, tiled=True)
    grad = lax.psum(grad, "ctx")
    update, m_norm, m_absmax, v_norm, v_absmax = adam_blocks(
        grad, m_codes, m_scales, v_codes, v_scales
    )
    return (dq, update, m_norm, m_absmax, v_norm, v_absmax)


def solution(mesh):
    in_specs = (
        P("dp", "ctx", None),
        P("dp", "ctx", None),
        P("dp", "ctx", None),
        P("dp", "ctx", None),
        P("dp", "ctx", None),
        P("dp", None),
        P(),
        P("dp", None),
        P("dp"),
        P("dp", None),
        P("dp"),
    )
    out_specs = (
        P("dp", "ctx", None),
        P("dp", None),
        P("dp", None),
        P("dp"),
        P("dp", None),
        P("dp"),
    )
    return jax.shard_map(shards, mesh=mesh, in_specs=in_specs, out_specs=out_specs, check_vma=False)
```

profile of v0, /device:TPU:32, one launch (start us, length us, event | category | flops | bytes accessed | tf_op | source)
XLA Modules:
  0.0 549.1 jit_solution(15692817767166467675)
XLA Ops:
  11.0 29.1 %all-gather = bf16[1,1536,128]{2,1,0:T(8,128)(2,1)S(1)} all-gather(bf16[1,192,128]{2,1,0:T(8,128)(2,1)} %param.16), channel_id=2, replica_groups=mesh['dp'=32,'ctx'=8] {'ctx'}, dimensions={1}, use_global_device_ids=true | all-gather | bytes 442368 | tf_op jit(solution)/shard_map/all_gather | solution.py:71
  41.5 30.8 %all-gather.1 = bf16[1,1536,128]{2,1,0:T(8,128)(2,1)} all-gather(bf16[1,192,128]{2,1,0:T(8,128)(2,1)} %param.17), channel_id=3, replica_groups=mesh['dp'=32,'ctx'=8] {'ctx'}, dimensions={1}, use_global_device_ids=true | all-gather | bytes 442368 | tf_op jit(solution)/shard_map/all_gather | solution.py:72
  72.7 46.8 %while.28 = (s32[]{:T(128)}, f32[3072,1]{0,1:T(1,128)}, f32[3072,1]{0,1:T(1,128)}, f32[3072,1]{0,1:T(1,128)}, s32[3,512]{1,0:T(4,128)}, /*index=5*/s32[192]{0:T(...) while((s32[]{:T(128)}, f32[3072,1]{0,1:T(1,128)}, ...), condition=%wide.region_7.8_spmd.clone, body=%wide.region_3.7_spmd.clone.sunk | while | flops 824497152 | bytes 55990092 | solution.py:115
  74.7 1.7 copy.45
  76.4 3.9 fusion.79
  80.3 5.2 fusion.81
  89.8 1.7 copy.45
  91.5 3.9 fusion.79
  96.1 5.2 fusion.81
  107.3 3.8 fusion.79
  111.9 5.2 fusion.81
  120.9 55.8 %while.29 = (s32[]{:T(128)}, f32[3072,128]{1,0:T(8,128)}, f32[3,512,256]{2,1,0:T(8,128)}, s32[3,512]{1,0:T(4,128)}, s32[192]{0:T(256)S(1)}, /*index=5*/s32[3,512...) while((s32[]{:T(128)}, f32[3072,128]{1,0:T(8,128)}, ...), condition=%wide.region_9.10_spmd.clone, body=%wide.region_8.9_spmd.clone.sunk | while | flops 2027126784 | bytes 108267456 | solution.py:132
  123.0 1.7 copy.46
  124.7 1.9 fusion.94
  126.7 2.9 fusion.95
  129.7 2.2 convolution_add_fusion.2
  133.0 2.3 fusion.96
  135.3 2.3 convolution_multiply_fusion.2
  143.0 1.9 fusion.94
  145.0 2.9 fusion.95
  148.0 3.8 convolution_add_fusion.2
  151.7 2.3 fusion.96
  154.1 2.3 convolution_multiply_fusion.2
  161.8 1.9 fusion.94
  163.7 2.9 fusion.95
  166.7 3.8 convolution_add_fusion.2
  170.5 2.3 fusion.96
  172.8 2.3 convolution_multiply_fusion.2
  176.7 49.4 %reduce-scatter.3.cloned.1.call-done = f32[192,256]{1,0:T(8,128)} async-done(((f32[1536,256]{1,0:T(8,128)}), f32[192,256]{1,0:T(8,128)}) %reduce-scatter.3.cloned.1.call-update) | async-done | bytes 196624 | tf_op jit(solution)/shard_map/reduce_scatter | solution.py:137
  226.2 11.0 %convolution_bitcast_fusion = f32[16384,256]{0,1:T(8,128)} fusion(bf16[1,192,16384]{2,1,0:T(8,128)(2,1)} %param.19, f32[192,256]{1,0:T(8,128)} %reduce-scatter.3.cloned.1.call-done), kind=kOutput, calls=%fused_computation.49 | convolution fusion | flops 1610661888 | bytes 23265280 | tf_op jit(solution)/shard_map/dot_general | solution.py:40
  237.3 218.4 %reduce-scatter.5.cloned.1.call-done = f32[512,256]{0,1:T(8,128)} async-done(((f32[16384,256]{0,1:T(8,128)}), f32[512,256]{0,1:T(8,128)}) %reduce-scatter.5.cloned.1.call-update) | async-done | bytes 524304 | tf_op jit(solution)/shard_map/reduce_scatter | solution.py:140
  457.9 79.3 %all-reduce.2.cloned.1.call-done = f32[512,256]{0,1:T(8,128)} async-done(((f32[512,256]{0,1:T(8,128)}), f32[512,256]{0,1:T(8,128)}) %all-reduce.2.cloned.1.call-update) | async-done | bytes 524304 | tf_op jit(solution)/shard_map/psum | solution.py:141
  (197 shorter events, 45.8 us)
Async XLA Ops:
  7.2 65.2 %copy-start.10 = (bf16[1,192,2048]{2,1,0:T(8,128)(2,1)S(1)}, bf16[1,192,2048]{2,1,0:T(8,128)(2,1)}, u32[]{:S(2)}) copy-start(bf16[1,192,2048]{2,1,0:T(8,128)(2,1)} %param.18) | copy-start | bytes 2359300
  7.2 219.0 %reduce-scatter.3.cloned.1.call-start = ((), (), s32[]{:S(2)}) async-start(), calls=%async_computation.2 | async-start | bytes 1769472 | tf_op jit(solution)/shard_map/reduce_scatter | solution.py:137
  80.3 5.2 copy-start
  96.1 5.2 copy-start
  111.9 5.2 copy-start
  120.9 5.8 %copy-start.4 = (bf16[3072,128]{1,0:T(8,128)(2,1)}, bf16[3072,128]{1,0:T(8,128)(2,1)S(1)}, u32[]{:S(2)}) copy-start(bf16[3072,128]{1,0:T(8,128)(2,1)S(1)} %get-tuple-element.577) | copy-start | bytes 2359300 | tf_op jit(solution)/shard_map/while
  120.9 5.8 %copy-start.6 = (bf16[3072,128]{1,0:T(8,128)(2,1)}, bf16[3072,128]{1,0:T(8,128)(2,1)S(1)}, u32[]{:S(2)}) copy-start(bf16[3072,128]{1,0:T(8,128)(2,1)S(1)} %get-tuple-element.581) | copy-start | bytes 2359300 | tf_op jit(solution)/shard_map/while
  120.9 3.8 copy-start.9
  120.9 3.8 copy-start.16
  126.7 3.0 copy-start.1
  129.7 3.4 copy-start.2
  139.2 5.8 %copy-start.4 = (bf16[3072,128]{1,0:T(8,128)(2,1)}, bf16[3072,128]{1,0:T(8,128)(2,1)S(1)}, u32[]{:S(2)}) copy-start(bf16[3072,128]{1,0:T(8,128)(2,1)S(1)} %get-tuple-element.577) | copy-start | bytes 2359300 | tf_op jit(solution)/shard_map/while
  139.2 5.8 %copy-start.6 = (bf16[3072,128]{1,0:T(8,128)(2,1)}, bf16[3072,128]{1,0:T(8,128)(2,1)S(1)}, u32[]{:S(2)}) copy-start(bf16[3072,128]{1,0:T(8,128)(2,1)S(1)} %get-tuple-element.581) | copy-start | bytes 2359300 | tf_op jit(solution)/shard_map/while
  139.2 3.8 copy-start.9
  139.2 3.8 copy-start.16
  145.0 3.0 copy-start.1
  148.0 3.8 copy-start.2
  157.9 5.8 %copy-start.4 = (bf16[3072,128]{1,0:T(8,128)(2,1)}, bf16[3072,128]{1,0:T(8,128)(2,1)S(1)}, u32[]{:S(2)}) copy-start(bf16[3072,128]{1,0:T(8,128)(2,1)S(1)} %get-tuple-element.577) | copy-start | bytes 2359300 | tf_op jit(solution)/shard_map/while
  157.9 5.8 %copy-start.6 = (bf16[3072,128]{1,0:T(8,128)(2,1)}, bf16[3072,128]{1,0:T(8,128)(2,1)S(1)}, u32[]{:S(2)}) copy-start(bf16[3072,128]{1,0:T(8,128)(2,1)S(1)} %get-tuple-element.581) | copy-start | bytes 2359300 | tf_op jit(solution)/shard_map/while
  157.9 3.8 copy-start.9
  157.9 3.8 copy-start.16
  163.7 3.0 copy-start.1
  166.7 3.8 copy-start.2
  176.7 279.0 %reduce-scatter.5.cloned.1.call-start = ((), (), s32[]{:S(2)}) async-start(), calls=%async_computation.3 | async-start | bytes 17301504 | tf_op jit(solution)/shard_map/reduce_scatter | solution.py:140
  237.2 218.6 %copy-start.3 = (f32[3072,128]{1,0:T(8,128)S(1)}, f32[3072,128]{1,0:T(8,128)}, u32[]{:S(2)}) copy-start(f32[3072,128]{1,0:T(8,128)} %get-tuple-element.146) | copy-start | bytes 4718596
  237.2 219.9 %copy-start.21 = (f32[64]{0:T(128)S(1)}, f32[64]{0:T(128)}, u32[]{:S(2)}) copy-start(f32[64]{0:T(128)} %param.23) | copy-start | bytes 772
  237.2 220.1 %copy-start.11 = (s32[512,256]{1,0:T(8,128)S(1)}, s32[512,256]{1,0:T(8,128)}, u32[]{:S(2)}) copy-start(s32[512,256]{1,0:T(8,128)} %param.22) | copy-start | bytes 1572868
  237.2 220.3 %copy-start.22 = (f32[64]{0:T(128)S(1)}, f32[64]{0:T(128)}, u32[]{:S(2)}) copy-start(f32[64]{0:T(128)} %param.25) | copy-start | bytes 772
  237.2 220.4 %copy-start.12 = (s32[512,256]{1,0:T(8,128)S(1)}, s32[512,256]{1,0:T(8,128)}, u32[]{:S(2)}) copy-start(s32[512,256]{1,0:T(8,128)} %param.24) | copy-start | bytes 1572868
  237.2 300.0 %all-reduce.2.cloned.1.call-start = ((), (), s32[]{:S(2)}) async-start(), calls=%async_computation.4 | async-start | bytes 1048576 | tf_op jit(solution)/shard_map/psum | solution.py:141
  538.7 3.9 copy-start.19
  539.1 3.5 copy-start.20
  (24 other events, 33.0 us)
Sparse Core Ops, SparseCore 0:
  176.8 49.3 reduce-scatter.2
  237.3 218.3 reduce-scatter.4
  458.5 78.6 all-reduce.1
where the time goes:
time: 550 us; the launch traced here: 549 us
  waiting for transfers between devices  347 us (63%)
  matrix products  76.2 us (14%)
  blocking collectives  59.9 us (11%)
  local copies, waits for them, and re-layouts  33.6 us (6%)
  other arithmetic  17.2 us (3%)
  between operations  14 us (3%)
    reduce_scatter x1, waiting for transfers between devices, shards(): lax.psum_scatter(contract_rows(layer_in, own_low), 'dp', scatter_dimensio...  218 us
    psum x1, waiting for transfers between devices, shards(): grad = lax.psum(grad, 'ctx')  79.3 us
    reduce_scatter x1, waiting for transfers between devices, shards(): lax.psum_scatter(partial_grads, 'ctx', scatter_dimension=0, tiled=True)  49.4 us
    dot_general x12, matrix products, contract_cols(): lax.dot_general(left, right, (((1,), (1,)), ((), ())), preferred_element_...  41.6 us
    all_gather x1, blocking collectives, shards(): lax.all_gather(values[0], 'ctx', axis=0, tiled=True)  30.8 us
    all_gather x1, blocking collectives, shards(): lax.all_gather(keys[0], 'ctx', axis=0, tiled=True)  29.1 us
    dot_general x7, matrix products, contract_rows(): lax.dot_general(left, right, (((0,), (0,)), ((), ())), preferred_element_...  24.8 us
  transfers between devices with their start and end apart: 3, of which 3 were waited for; matrix products, arithmetic and copies ran while one was open for 0% of the time, Pallas kernels for 0%

commit v1 on v0

--- a/solution.py
+++ b/solution.py
@@ -6,6 +6,11 @@
 
 BLOCK = 2048
 STEP = 10
+
+
+def gather_and_add(x, name):
+    terms = lax.all_gather(x, name)
+    return jnp.sum(terms, axis=0)
 
 
 def positions(order, span, total):
@@ -138,7 +143,7 @@
     own_low = own.astype(jnp.bfloat16)
     layer_in = hidden_in[0]
     grad = lax.psum_scatter(contract_rows(layer_in, own_low), "dp", scatter_dimension=0, tiled=True)
-    grad = lax.psum(grad, "ctx")
+    grad = gather_and_add(grad, "ctx")
     update, m_norm, m_absmax, v_norm, v_absmax = adam_blocks(
         grad, m_codes, m_scales, v_codes, v_scales
     )

time: 550 us -> 578 us (1.051)
  waiting for transfers between devices: 347 us -> 359 us
  matrix products: 76.2 us -> 83.3 us
    all_gather x0 -> x1, waiting for transfers between devices: none -> 91.1 us  [gather_and_add(): terms = lax.all_gather(x, name)]
    psum x1 -> x0, waiting for transfers between devices: 79.3 us -> none  [shards(): grad = lax.psum(grad, 'ctx')]
    dot_general x12, matrix products: 41.6 us -> 48.8 us  [contract_cols(): lax.dot_general(left, right, (((1,), (1,)), ((), ())), preferred_element_...]
    unnamed x21 -> x20, local copies, waits for them, and re-layouts: 3.42 us -> 9.4 us
where the time goes in v1:
time: 578 us; the launch traced here: 574 us
  waiting for transfers between devices  359 us (62%)
  matrix products  83.3 us (14%)
  blocking collectives  59.9 us (10%)
  local copies, waits for them, and re-layouts  38.4 us (7%)
  other arithmetic  18.9 us (3%)
  between operations  14 us (2%)
    reduce_scatter x1, waiting for transfers between devices, shards(): lax.psum_scatter(contract_rows(layer_in, own_low), 'dp', scatter_dimensio...  219 us
    all_gather x1, waiting for transfers between devices, gather_and_add(): terms = lax.all_gather(x, name)  91.1 us
    reduce_scatter x1, waiting for transfers between devices, shards(): lax.psum_scatter(partial_grads, 'ctx', scatter_dimension=0, tiled=True)  49.2 us
    dot_general x12, matrix products, contract_cols(): lax.dot_general(left, right, (((1,), (1,)), ((), ())), preferred_element_...  48.8 us
    all_gather x1, blocking collectives, shards(): lax.all_gather(values[0], 'ctx', axis=0, tiled=True)  30.8 us
    all_gather x1, blocking collectives, shards(): lax.all_gather(keys[0], 'ctx', axis=0, tiled=True)  29.1 us
    dot_general x7, matrix products, contract_rows(): lax.dot_general(left, right, (((0,), (0,)), ((), ())), preferred_element_...  24.8 us
  transfers between devices with their start and end apart: 3, of which 3 were waited for; matrix products, arithmetic and copies ran while one was open for 0% of the time, Pallas kernels for 0%

profile of v1, /device:TPU:32, one launch (start us, length us, event | category | flops | bytes accessed | tf_op | source)
XLA Modules:
  0.0 574.3 jit_solution(10893409055551548766)
XLA Ops:
  10.9 29.1 %all-gather = bf16[1,1536,128]{2,1,0:T(8,128)(2,1)S(1)} all-gather(bf16[1,192,128]{2,1,0:T(8,128)(2,1)} %param.16), channel_id=2, replica_groups=mesh['dp'=32,'ctx'=8] {'ctx'}, dimensions={1}, use_global_device_ids=true | all-gather | bytes 442368 | tf_op jit(solution)/shard_map/all_gather | solution.py:76
  40.0 2.2 reshape_squeeze.6
  42.2 30.8 %all-gather.1 = bf16[1,1536,128]{2,1,0:T(8,128)(2,1)} all-gather(bf16[1,192,128]{2,1,0:T(8,128)(2,1)} %param.17), channel_id=3, replica_groups=mesh['dp'=32,'ctx'=8] {'ctx'}, dimensions={1}, use_global_device_ids=true | all-gather | bytes 442368 | tf_op jit(solution)/shard_map/all_gather | solution.py:77
  73.0 2.2 reshape_squeeze.7
  75.2 50.5 %while.28 = (s32[]{:T(128)}, f32[3072,1]{0,1:T(1,128)S(1)}, f32[3072,1]{0,1:T(1,128)}, f32[3072,1]{0,1:T(1,128)S(1)}, s32[3,512]{1,0:T(4,128)}, /*index=5*/s32[1...) while((s32[]{:T(128)}, f32[3072,1]{0,1:T(1,128)S(1)}, ...), condition=%wide.region_7.8_spmd.clone, body=%wide.region_3.7_spmd.clone.sunk | while | flops 824497152 | bytes 55744192 | solution.py:120
  78.9 5.0 fusion.79
  83.9 5.4 fusion.81
  95.3 5.0 fusion.79
  100.3 5.3 fusion.81
  112.3 5.0 fusion.79
  117.4 5.4 fusion.81
  127.1 56.8 %while.29 = (s32[]{:T(128)}, f32[3072,128]{1,0:T(8,128)}, f32[3,512,256]{2,1,0:T(8,128)}, s32[3,512]{1,0:T(4,128)}, s32[192]{0:T(256)S(1)}, /*index=5*/s32[3,512...) while((s32[]{:T(128)}, f32[3072,128]{1,0:T(8,128)}, ...), condition=%wide.region_9.10_spmd.clone, body=%wide.region_8.9_spmd.clone.sunk | while | flops 2027126784 | bytes 95536888 | solution.py:137
  130.8 3.1 fusion.94
  133.9 2.8 fusion.95
  136.7 2.2 convolution_add_fusion.2
  140.0 2.3 fusion.96
  142.4 2.3 convolution_multiply_fusion.2
  149.4 3.1 fusion.94
  152.5 2.8 fusion.95
  155.4 3.7 convolution_add_fusion.2
  159.1 2.3 fusion.96
  161.4 2.3 convolution_multiply_fusion.2
  168.5 3.1 fusion.94
  171.6 2.8 fusion.95
  174.5 3.7 convolution_add_fusion.2
  178.2 2.3 fusion.96
  180.5 2.3 convolution_multiply_fusion.2
  184.0 49.2 %reduce-scatter.3.cloned.1.call-done = f32[192,256]{1,0:T(8,128)} async-done(((f32[1536,256]{1,0:T(8,128)}), f32[192,256]{1,0:T(8,128)}) %reduce-scatter.3.cloned.1.call-update) | async-done | bytes 196624 | tf_op jit(solution)/shard_map/reduce_scatter | solution.py:142
  233.2 11.0 %convolution_bitcast_fusion = f32[16384,256]{0,1:T(8,128)} fusion(bf16[1,192,16384]{2,1,0:T(8,128)(2,1)} %param.19, f32[192,256]{1,0:T(8,128)} %reduce-scatter.3.cloned.1.call-done), kind=kOutput, calls=%fused_computation.49 | convolution fusion | flops 1610661888 | bytes 23265280 | tf_op jit(solution)/shard_map/dot_general | solution.py:45
  244.5 218.7 %reduce-scatter.5.cloned.1.call-done = f32[512,256]{0,1:T(8,128)} async-done(((f32[16384,256]{0,1:T(8,128)}), f32[512,256]{0,1:T(8,128)}) %reduce-scatter.5.cloned.1.call-update) | async-done | bytes 524304 | tf_op jit(solution)/shard_map/reduce_scatter | solution.py:145
  465.4 91.1 %all-gather.5.cloned.1.call-done = f32[4096,256]{0,1:T(8,128)} async-done(((f32[512,256]{0,1:T(8,128)}), f32[4096,256]{0,1:T(8,128)}) %all-gather.5.cloned.1.call-update) | async-done | bytes 4194320 | tf_op jit(solution)/shard_map/all_gather | solution.py:12
  556.5 6.0 %copy.42 = f32[32,8,8,512]{3,2,1,0:T(8,128)S(1)} copy(f32[32,8,8,512]{3,1,2,0:T(8,128)} %bitcast.150) | data formatting | bytes 8388608
  (125 shorter events, 47.3 us)
Async XLA Ops:
  7.2 226.0 %reduce-scatter.3.cloned.1.call-start = ((), (), s32[]{:S(2)}) async-start(), calls=%async_computation.2 | async-start | bytes 1769472 | tf_op jit(solution)/shard_map/reduce_scatter | solution.py:142
  83.9 5.4 copy-start
  100.3 5.4 copy-start
  117.4 5.4 copy-start
  133.8 2.8 copy-start.1
  136.7 3.4 copy-start.2
  152.5 2.8 copy-start.1
  155.4 3.8 copy-start.2
  171.6 2.8 copy-start.1
  174.5 3.8 copy-start.2
  183.9 279.3 %reduce-scatter.5.cloned.1.call-start = ((), (), s32[]{:S(2)}) async-start(), calls=%async_computation.3 | async-start | bytes 17301504 | tf_op jit(solution)/shard_map/reduce_scatter | solution.py:145
  244.2 219.1 %copy-start.3 = (f32[3072,128]{1,0:T(8,128)S(1)}, f32[3072,128]{1,0:T(8,128)}, u32[]{:S(2)}) copy-start(f32[3072,128]{1,0:T(8,128)} %get-tuple-element.146) | copy-start | bytes 4718596
  244.2 220.4 %copy-start.8 = (f32[64]{0:T(128)S(1)}, f32[64]{0:T(128)}, u32[]{:S(2)}) copy-start(f32[64]{0:T(128)} %param.23) | copy-start | bytes 772
  244.2 220.6 %copy-start.4 = (s32[512,256]{1,0:T(8,128)S(1)}, s32[512,256]{1,0:T(8,128)}, u32[]{:S(2)}) copy-start(s32[512,256]{1,0:T(8,128)} %param.22) | copy-start | bytes 1572868
  244.2 220.8 %copy-start.9 = (f32[64]{0:T(128)S(1)}, f32[64]{0:T(128)}, u32[]{:S(2)}) copy-start(f32[64]{0:T(128)} %param.25) | copy-start | bytes 772
  244.2 220.9 %copy-start.5 = (s32[512,256]{1,0:T(8,128)S(1)}, s32[512,256]{1,0:T(8,128)}, u32[]{:S(2)}) copy-start(s32[512,256]{1,0:T(8,128)} %param.24) | copy-start | bytes 1572868
  244.2 312.2 %all-gather.5.cloned.1.call-start = ((), (), s32[]{:S(2)}) async-start(), calls=%async_computation.4 | async-start | bytes 4718592 | tf_op jit(solution)/shard_map/all_gather | solution.py:12
  563.9 3.9 copy-start.6
  564.3 3.5 copy-start.7
Sparse Core Ops, SparseCore 0:
  184.1 49.0 reduce-scatter.2
  244.3 218.8 reduce-scatter.4
  465.1 91.2 all-gather.4
